TPU v7x, 32 devices: a whole 2x2x4 slice. The times are simulated.
32 devices in a mesh: pipe: 2 (over core), dp: 16 (over z, y, x).
Axes of the slice: x: 2, y: 2, z: 4, core: 2. Of those that a mesh axis runs over, the one named last changes fastest.
Arguments:
- gate: bfloat16 [2, 1, 2048, 4096], P('pipe', None, 'dp'), may hold values from -5 to 5
- filters: bfloat16 [2, 256, 128], P('pipe', 'dp'), may hold values from -0.75 to 0.75
- doc_ids: int32 [1, 2048], P(None, 'dp'), may hold values from 0 to 1, as said below
- loss_grad: bfloat16 [1, 2048, 4096], P(None, 'dp'), may hold values from -6 to 6
Outputs:
- input_grads: bfloat16 [2, 1, 2048, 4096], P('pipe', None, 'dp')
Inputs may be any that keep to these rules, and one draw needn't show every extreme that they name: `doc_ids`: within each window the ids never fall, begin at 0 and end at 1, and every document holds 128 or more tokens.
All inputs are finite; a program needn't handle non-finite values.
Results may differ from a plain program's by a relative error of at most 0.0049.
Values may be sent and summed in bfloat16 or wider, within the bound.
A program may use at most 64 MiB of HBM per device.

v0:
```python
import jax
import jax.numpy as jnp
from jax import lax
from jax.sharding import PartitionSpec as P


def passed_along(value, axis, by):
    count = lax.axis_size(axis)
    pairs = [(i, i + by) for i in range(count) if 0 <= i + by < count]
    return lax.ppermute(value, axis, pairs)


def band_table(filt_block, tap_count):
    groups = filt_block.shape[0]
    span_cols = 2 * tap_count
    base_row = jnp.concatenate(
        [filt_block, jnp.zeros((groups, span_cols + 1 - tap_count), filt_block.dtype)], axis=1
    )
    tiled_rows = jnp.broadcast_to(base_row[:, None, :], (groups, tap_count, span_cols + 1))
    tiled_rows = tiled_rows.reshape(groups, tap_count * (span_cols + 1))
    return tiled_rows[:, : tap_count * span_cols].reshape(groups, tap_count, span_cols)


def adjoint_block(filt_all, scaled_own, scaled_head, parity_own, parity_head):
    row_count, channels = scaled_own.shape
    groups, tap_count = filt_all.shape
    lane_width = channels // groups
    group_block = 64
    block_count = groups // group_block
    row_blocks = row_count // tap_count
    window = jnp.concatenate([scaled_own, scaled_head], axis=0)
    window_parity = jnp.concatenate([parity_own, parity_head], axis=0)
    arranged = window.reshape(
        row_count + tap_count, block_count, group_block, lane_width
    ).transpose(1, 0, 2, 3)
    front_rows = arranged[:, :row_count].reshape(
        block_count, row_blocks, tap_count, group_block, lane_width
    )
    behind = arranged[:, tap_count:].reshape(
        block_count, row_blocks, tap_count, group_block, lane_width
    )
    slabs = jnp.concatenate([front_rows, behind], axis=2)
    column_parity = jnp.concatenate(
        [
            window_parity[:row_count].reshape(row_blocks, tap_count),
            window_parity[tap_count:].reshape(row_blocks, tap_count),
        ],
        axis=1,
    )
    same_doc = parity_own.reshape(row_blocks, tap_count)[:, :, None] == column_parity[:, None, :]
    filt_blocks = filt_all.reshape(block_count, group_block, tap_count)

    def one_block(inputs):
        filt_part, slab_piece = inputs
        band_rows = band_table(filt_part, tap_count)
        masked = jnp.where(same_doc[:, None], band_rows[None], jnp.zeros((), band_rows.dtype))
        return jnp.einsum("rgtj,rjgc->rtgc", masked, slab_piece, preferred_element_type=jnp.float32)

    product = lax.map(one_block, (filt_blocks, slabs))
    return product.transpose(1, 2, 0, 3, 4).reshape(row_count, channels)


def body(gate, filters, doc_ids, loss_grad):
    gate_local = gate[0]
    micro_count, row_count, channels = gate_local.shape
    filt_all = lax.all_gather(filters, "dp", axis=1, tiled=True)[0]
    tap_count = filt_all.shape[1]
    section_count = lax.axis_size("pipe")
    section_index = lax.axis_index("pipe")
    parity = doc_ids % 2
    tick_count = micro_count + section_count - 1
    is_last = section_index == section_count - 1
    is_first = section_index == 0

    def one_tick(tick, carry):
        payload, results = carry
        received = passed_along(payload, "pipe", -1)
        micro_index = tick - (section_count - 1 - section_index)
        active = jnp.logical_and(micro_index >= 0, micro_index < micro_count)
        chosen = jnp.clip(micro_index, 0, micro_count - 1)
        own_loss = lax.dynamic_index_in_dim(loss_grad, chosen, 0, keepdims=False)
        incoming = jnp.where(is_last, own_loss, received)
        gate_now = lax.dynamic_index_in_dim(gate_local, chosen, 0, keepdims=False)
        parity_now = lax.dynamic_index_in_dim(parity, chosen, 0, keepdims=False)
        scaled = (gate_now.astype(jnp.float32) * incoming.astype(jnp.float32)).astype(jnp.bfloat16)
        scaled_head, parity_head = passed_along((scaled, parity_now), "dp", -1)

        def working(unused):
            update = adjoint_block(filt_all, scaled, scaled_head, parity_now, parity_head)
            return (incoming.astype(jnp.float32) + update).astype(jnp.bfloat16)

        def waiting(unused):
            return jnp.zeros_like(incoming)

        produced = lax.cond(active, working, waiting, 0)
        previous = lax.dynamic_index_in_dim(results, chosen, 0, keepdims=False)
        results = lax.dynamic_update_index_in_dim(
            results, jnp.where(active, produced, previous), chosen, 0
        )
        following = jnp.clip(tick + 1, 0, micro_count - 1)
        next_loss = lax.dynamic_index_in_dim(loss_grad, following, 0, keepdims=False)
        payload = jnp.where(is_first, next_loss, produced)
        return (payload, results)

    start_payload = jnp.where(is_first, loss_grad[0], jnp.zeros_like(loss_grad[0]))
    start_results = jnp.zeros_like(gate_local)
    _, results = lax.fori_loop(0, tick_count, one_tick, (start_payload, start_results))
    return results[None]


def solution(mesh):
    return jax.shard_map(
        body,
        mesh=mesh,
        in_specs=(
            P("pipe", None, "dp", None),
            P("pipe", "dp", None),
            P(None, "dp"),
            P(None, "dp", None),
        ),
        out_specs=P("pipe", None, "dp", None),
        check_vma=False,
    )
```

profile of v0, /device:TPU:0, one launch (start us, length us, event | category | flops | bytes accessed | tf_op | source)
XLA Modules:
  0.0 292.6 jit_solution(9645054348732942074)
XLA Ops:
  5.4 43.9 %all_gather.3 = bf16[1,256,128]{2,1,0:T(8,128)(2,1)S(1)} all-gather(bf16[1,16,128]{2,1,0:T(8,128)(2,1)S(1)} %copy-done.1), channel_id=1, replica_groups=mesh['pipe'=2,'dp'=16] {'dp'}, dimensions={1}, use_global_device_ids=true | all-gather | bytes 69632 | tf_op jit(solution)/shard_map/all_gather | solution.py:66
  51.7 238.6 %while.28 = (s32[]{:T(128)}, bf16[128,4096]{0,1:T(8,128)(2,1)}, bf16[1,128,4096]{1,2,0:T(8,128)(2,1)}, pred[]{:T(512)}, bf16[1,128,4096]{1,2,0:T(8,128)(2,1)S(1)...) while((s32[]{:T(128)}, bf16[128,4096]{0,1:T(8,128)(2,1)}, ...), condition=%wide.region_5.6_spmd, body=%wide.region_0.5_spmd.sunk | while | flops 82870536 | bytes 83072224 | solution.py:107
  53.0 3.5 %collective-permute-done = bf16[128,4096]{0,1:T(8,128)(2,1)S(1)} collective-permute-done((bf16[128,4096]{0,1:T(8,128)(2,1)}, bf16[128,4096]{0,1:T(8,128)(2,1)S(1)}, u32[]{:S(2)}, u32[]{:S(2)}) %collective-permute-start) | collective-permute-done | bytes 1048608 | tf_op jit(solution)/shard_map/while/body/eval_jaxpr/ppermute | solution.py:10
  56.5 2.7 fusion.17
  60.4 25.8 %collective-permute-done.1 = bf16[128,4096]{0,1:T(8,128)(2,1)S(1)} collective-permute-done((bf16[128,4096]{0,1:T(8,128)(2,1)S(1)}, bf16[128,4096]{0,1:T(8,128)(2,1)S(1)}, u32[]{:S(2)}, u32[]{:S(2)}) %collective-permute-start.1) | collective-permute-done | bytes 1048608 | tf_op jit(solution)/shard_map/while/body/eval_jaxpr/ppermute | solution.py:10
  86.4 2.7 fusion.18
  90.4 84.5 %collective-permute-done = bf16[128,4096]{0,1:T(8,128)(2,1)S(1)} collective-permute-done((bf16[128,4096]{0,1:T(8,128)(2,1)}, bf16[128,4096]{0,1:T(8,128)(2,1)S(1)}, u32[]{:S(2)}, u32[]{:S(2)}) %collective-permute-start) | collective-permute-done | bytes 1048608 | tf_op jit(solution)/shard_map/while/body/eval_jaxpr/ppermute | solution.py:10
  174.9 2.7 fusion.17
  178.8 25.8 %collective-permute-done.1 = bf16[128,4096]{0,1:T(8,128)(2,1)S(1)} collective-permute-done((bf16[128,4096]{0,1:T(8,128)(2,1)S(1)}, bf16[128,4096]{0,1:T(8,128)(2,1)S(1)}, u32[]{:S(2)}, u32[]{:S(2)}) %collective-permute-start.1) | collective-permute-done | bytes 1048608 | tf_op jit(solution)/shard_map/while/body/eval_jaxpr/ppermute | solution.py:10
  204.6 83.0 %conditional.2 = (bf16[128,4096]{0,1:T(8,128)(2,1)S(1)}) conditional(s32[]{:T(128)} %convert_element_type.55, () %tuple.66, (bf16[128,4096]{0,1:T(8,128)(2,1)}, bf16[1,256,128]{2,1,0:T(8,128)(2,1)S(1)}, bf16[128,4096]{0,1:T(8,128)(2,1)S(1)}, bf16[128,4096]{0,1:T(8,128)(2,1)S(1)}, s32[1,128]{1,0:T(1,128)S(1)}, /*index=5*/s32[128]{0:T(128)S(1)}) %tuple.67), branch_computations={%region_1.1_spmd, %region_2.4_spmd} | conditional | flops 79200512 | bytes 64197568 | solution.py:95
  205.5 80.0 %while.27 = (s32[]{:T(128)}, f32[4,1,128,64,16]{2,4,3,1,0:T(8,128)}, bf16[4,1,256,64,16]{2,4,3,1,0:T(8,128)(2,1)S(1)}, bf16[4,64,128]{2,1,0:T(8,128)(2,1)S(1)}, ...) while((s32[]{:T(128)}, f32[4,1,128,64,16]{2,4,3,1,0:T(8,128)}, ...), condition=%wide.region_4.3_spmd.clone, body=%wide.region_3.2_spmd.clone.sunk | while | flops 69238784 | bytes 47418224 | solution.py:59
  205.6 3.2 %broadcast_in_dim.53 = bf16[64,128,257]{2,1,0:T(8,128)(2,1)} broadcast(bf16[64,257]{1,0:T(8,128)(2,1)S(1)} %concatenate.14), dimensions={0,2} | broadcast | bytes 4243584 | tf_op jit(solution)/shard_map/while/body/eval_jaxpr/cond/branch_1_fun/while/body/eval_jaxpr/broadcast_in_dim | solution.py:19
  208.8 10.8 %reshape.107 = bf16[64,32896]{1,0:T(8,128)(2,1)} reshape(bf16[64,128,257]{2,1,0:T(8,128)(2,1)} %broadcast_in_dim.53) | data formatting | bytes 8421376 | tf_op jit(solution)/shard_map/while/body/eval_jaxpr/cond/branch_1_fun/while/body/eval_jaxpr/reshape | solution.py:20
  219.6 2.2 slice-done
  225.6 3.2 %broadcast_in_dim.53 = bf16[64,128,257]{2,1,0:T(8,128)(2,1)} broadcast(bf16[64,257]{1,0:T(8,128)(2,1)S(1)} %concatenate.14), dimensions={0,2} | broadcast | bytes 4243584 | tf_op jit(solution)/shard_map/while/body/eval_jaxpr/cond/branch_1_fun/while/body/eval_jaxpr/broadcast_in_dim | solution.py:19
  228.8 10.8 %reshape.107 = bf16[64,32896]{1,0:T(8,128)(2,1)} reshape(bf16[64,128,257]{2,1,0:T(8,128)(2,1)} %broadcast_in_dim.53) | data formatting | bytes 8421376 | tf_op jit(solution)/shard_map/while/body/eval_jaxpr/cond/branch_1_fun/while/body/eval_jaxpr/reshape | solution.py:20
  239.6 2.2 slice-done
  245.6 3.2 %broadcast_in_dim.53 = bf16[64,128,257]{2,1,0:T(8,128)(2,1)} broadcast(bf16[64,257]{1,0:T(8,128)(2,1)S(1)} %concatenate.14), dimensions={0,2} | broadcast | bytes 4243584 | tf_op jit(solution)/shard_map/while/body/eval_jaxpr/cond/branch_1_fun/while/body/eval_jaxpr/broadcast_in_dim | solution.py:19
  248.8 10.8 %reshape.107 = bf16[64,32896]{1,0:T(8,128)(2,1)} reshape(bf16[64,128,257]{2,1,0:T(8,128)(2,1)} %broadcast_in_dim.53) | data formatting | bytes 8421376 | tf_op jit(solution)/shard_map/while/body/eval_jaxpr/cond/branch_1_fun/while/body/eval_jaxpr/reshape | solution.py:20
  259.6 2.2 slice-done
  265.6 3.2 %broadcast_in_dim.53 = bf16[64,128,257]{2,1,0:T(8,128)(2,1)} broadcast(bf16[64,257]{1,0:T(8,128)(2,1)S(1)} %concatenate.14), dimensions={0,2} | broadcast | bytes 4243584 | tf_op jit(solution)/shard_map/while/body/eval_jaxpr/cond/branch_1_fun/while/body/eval_jaxpr/broadcast_in_dim | solution.py:19
  268.8 10.8 %reshape.107 = bf16[64,32896]{1,0:T(8,128)(2,1)} reshape(bf16[64,128,257]{2,1,0:T(8,128)(2,1)} %broadcast_in_dim.53) | data formatting | bytes 8421376 | tf_op jit(solution)/shard_map/while/body/eval_jaxpr/cond/branch_1_fun/while/body/eval_jaxpr/reshape | solution.py:20
  287.6 2.7 fusion.18
  290.4 2.3 copy.14
  (53 shorter events, 33.4 us)
Async XLA Ops:
  0.7 49.9 %collective-permute-start.2 = (s32[128]{0:T(128)S(1)}, s32[128]{0:T(128)S(1)}, u32[]{:S(2)}, u32[]{:S(2)}) collective-permute-start(s32[128]{0:T(128)S(1)} %fusion.11), channel_id=1, source_target_pairs={{1,0},{2,1},{3,2},{4,3},{5,4},{6,5},{7,6},{8,7},{9,8},{10,9},{11,1... | collective-permute-start | bytes 1544 | tf_op jit(solution)/shard_map/while/body/eval_jaxpr/ppermute | solution.py:10
  2.6 2.8 copy-start.1
  2.6 46.6 %copy-start = (bf16[1,1,128,4096]{3,2,1,0:T(8,128)(2,1)S(1)}, bf16[1,1,128,4096]{3,2,1,0:T(8,128)(2,1)}, u32[]{:S(2)}) copy-start(bf16[1,1,128,4096]{3,2,1,0:T(8,128)(2,1)} %param.10) | copy-start | bytes 3145732
  51.7 4.8 %collective-permute-start = (bf16[128,4096]{0,1:T(8,128)(2,1)}, bf16[128,4096]{0,1:T(8,128)(2,1)S(1)}, u32[]{:S(2)}, u32[]{:S(2)}) collective-permute-start(bf16[128,4096]{0,1:T(8,128)(2,1)} %get-tuple-element.528), channel_id=1, source_target_pairs={{16,0},{17,1},{18,2},{19,3},{20,4},{21,5},{22,6},{23,7},{24,8},{25... | collective-permute-start | bytes 3145736 | tf_op jit(solution)/shard_map/while/body/eval_jaxpr/ppermute | solution.py:10
  59.1 27.1 %collective-permute-start.1 = (bf16[128,4096]{0,1:T(8,128)(2,1)S(1)}, bf16[128,4096]{0,1:T(8,128)(2,1)S(1)}, u32[]{:S(2)}, u32[]{:S(2)}) collective-permute-start(bf16[128,4096]{0,1:T(8,128)(2,1)S(1)} %get-tuple-element.481), channel_id=1, source_target_pairs={{1,0},{2,1},{3,2},{4,3},{5,4},{6,5},{7,6},{8,7},{9,8},{10,9},{11,1... | collective-permute-start | bytes 3145736 | tf_op jit(solution)/shard_map/while/body/eval_jaxpr/ppermute | solution.py:10
  89.1 85.8 %collective-permute-start = (bf16[128,4096]{0,1:T(8,128)(2,1)}, bf16[128,4096]{0,1:T(8,128)(2,1)S(1)}, u32[]{:S(2)}, u32[]{:S(2)}) collective-permute-start(bf16[128,4096]{0,1:T(8,128)(2,1)} %get-tuple-element.528), channel_id=1, source_target_pairs={{16,0},{17,1},{18,2},{19,3},{20,4},{21,5},{22,6},{23,7},{24,8},{25... | collective-permute-start | bytes 3145736 | tf_op jit(solution)/shard_map/while/body/eval_jaxpr/ppermute | solution.py:10
  177.5 27.1 %collective-permute-start.1 = (bf16[128,4096]{0,1:T(8,128)(2,1)S(1)}, bf16[128,4096]{0,1:T(8,128)(2,1)S(1)}, u32[]{:S(2)}, u32[]{:S(2)}) collective-permute-start(bf16[128,4096]{0,1:T(8,128)(2,1)S(1)} %get-tuple-element.481), channel_id=1, source_target_pairs={{1,0},{2,1},{3,2},{4,3},{5,4},{6,5},{7,6},{8,7},{9,8},{10,9},{11,1... | collective-permute-start | bytes 3145736 | tf_op jit(solution)/shard_map/while/body/eval_jaxpr/ppermute | solution.py:10
  219.6 2.2 slice-start
  239.6 2.2 slice-start
  259.6 2.2 slice-start
  279.6 2.2 slice-start
where the time goes:
time: 294 us; the launch traced here: 293 us
  waiting for transfers between devices  140 us (48%)
  local copies, waits for them, and re-layouts  76.3 us (26%)
  blocking collectives  43.9 us (15%)
  other arithmetic  18.2 us (6%)
  matrix products  8.04 us (3%)
  starting transfers between devices  6.4 us (2%)
    ppermute x5, waiting for transfers between devices, passed_along(): return lax.ppermute(value, axis, pairs)  140 us
    all_gather x1, blocking collectives, body(): filt_all = lax.all_gather(filters, 'dp', axis=1, tiled=True)[0]  43.9 us
    reshape x4, local copies, waits for them, and re-layouts, band_table(): tiled_rows = tiled_rows.reshape(groups, tap_count * (span_cols + 1))  43.4 us
    broadcast_in_dim x4, local copies, waits for them, and re-layouts, band_table(): jnp.broadcast_to(base_row[:, None, :], (groups, tap_count, span_cols + 1))  12.8 us
    slice x8, local copies, waits for them, and re-layouts, band_table(): tiled_rows[:, :tap_count * span_cols].reshape(groups, tap_count, span_cols)  8.75 us
    dot_general x4, matrix products, one_block(): jnp.einsum('rgtj,rjgc->rtgc', masked, slab_piece, preferred_element_type=...  8.04 us
    ppermute x5, starting transfers between devices, passed_along(): return lax.ppermute(value, axis, pairs)  6.4 us
  transfers between devices with their start and end apart: 5, of which 4 were waited for; matrix products, arithmetic and copies ran while one was open for 2% of the time, Pallas kernels for 0%

commit v1 on v0

--- a/solution.py
+++ b/solution.py
@@ -2,6 +2,27 @@
 import jax.numpy as jnp
 from jax import lax
 from jax.sharding import PartitionSpec as P
+
+
+def in_order(blocks, dim):
+    blocks = jnp.moveaxis(blocks, 0, dim)
+    shape = blocks.shape
+    return blocks.reshape(*shape[:dim], shape[dim] * shape[dim + 1], *shape[dim + 2 :])
+
+
+def doubled(array, axis):
+    devices, index = (lax.axis_size(axis), lax.axis_index(axis))
+    blocks, distance = (array[None], 1)
+    while distance < devices:
+        theirs = lax.ppermute(blocks, axis, [(i, i ^ distance) for i in range(devices)])
+        low = index & distance == 0
+        blocks = jnp.concatenate([jnp.where(low, blocks, theirs), jnp.where(low, theirs, blocks)])
+        distance *= 2
+    return blocks
+
+
+def collect(array, axis, dim):
+    return in_order(doubled(array, axis), dim)
 
 
 def passed_along(value, axis, by):
@@ -63,7 +84,7 @@
 def body(gate, filters, doc_ids, loss_grad):
     gate_local = gate[0]
     micro_count, row_count, channels = gate_local.shape
-    filt_all = lax.all_gather(filters, "dp", axis=1, tiled=True)[0]
+    filt_all = collect(filters, "dp", 1)[0]
     tap_count = filt_all.shape[1]
     section_count = lax.axis_size("pipe")
     section_index = lax.axis_index("pipe")

time: 294 us -> 266 us (0.905)
  blocking collectives: 43.9 us -> 0 us
  starting transfers between devices: 6.4 us -> 18.1 us
  waiting for transfers between devices: 140 us -> 143 us
    all_gather x1 -> x0, blocking collectives: 43.9 us -> none  [body(): filt_all = lax.all_gather(filters, 'dp', axis=1, tiled=True)[0]]
    ppermute x0 -> x4, starting transfers between devices: none -> 11.7 us  [doubled(): lax.ppermute(blocks, axis, [(i, i ^ distance) for i in range(devices)])]
    ppermute x0 -> x4, waiting for transfers between devices: none -> 3.01 us  [doubled(): lax.ppermute(blocks, axis, [(i, i ^ distance) for i in range(devices)])]
  transfers between devices with their start and end apart: 5 -> 9, of which waited for: 4 -> 7; matrix products, arithmetic and copies ran while one was open for 2% -> 2% of each run, Pallas kernels for 0% -> 0%
where the time goes in v1:
time: 266 us; the launch traced here: 264 us
  waiting for transfers between devices  143 us (54%)
  local copies, waits for them, and re-layouts  76.5 us (29%)
  other arithmetic  18.3 us (7%)
  starting transfers between devices  18.1 us (7%)
  matrix products  8.09 us (3%)
    ppermute x5, waiting for transfers between devices, passed_along(): return lax.ppermute(value, axis, pairs)  140 us
    reshape x4, local copies, waits for them, and re-layouts, band_table(): tiled_rows = tiled_rows.reshape(groups, tap_count * (span_cols + 1))  43.5 us
    broadcast_in_dim x4, local copies, waits for them, and re-layouts, band_table(): jnp.broadcast_to(base_row[:, None, :], (groups, tap_count, span_cols + 1))  12.8 us
    ppermute x4, starting transfers between devices, doubled(): lax.ppermute(blocks, axis, [(i, i ^ distance) for i in range(devices)])  11.7 us
    slice x8, local copies, waits for them, and re-layouts, band_table(): tiled_rows[:, :tap_count * span_cols].reshape(groups, tap_count, span_cols)  8.75 us
    dot_general x4, matrix products, one_block(): jnp.einsum('rgtj,rjgc->rtgc', masked, slab_piece, preferred_element_type=...  8.09 us
    ppermute x5, starting transfers between devices, passed_along(): return lax.ppermute(value, axis, pairs)  6.4 us
    broadcast_in_dim x2, other arithmetic, one_tick(): lax.dynamic_update_index_in_dim(results, jnp.where(active, produced, prev...  5.43 us
  transfers between devices with their start and end apart: 9, of which 7 were waited for; matrix products, arithmetic and copies ran while one was open for 2% of the time, Pallas kernels for 0%

profile of v1, /device:TPU:0, one launch (start us, length us, event | category | flops | bytes accessed | tf_op | source)
XLA Modules:
  0.0 264.3 jit_solution(3437398901802618344)
XLA Ops:
  0.0 2.9 %collective-permute-start.2 = (bf16[1,1,16,128]{3,2,0,1:T(8,128)(2,1)}, bf16[1,1,16,128]{3,2,0,1:T(8,128)(2,1)S(1)}, u32[]{:S(2)}, u32[]{:S(2)}) collective-permute-start(bf16[1,1,16,128]{3,2,0,1:T(8,128)(2,1)} %bitcast.86), channel_id=1, source_target_pairs={{0,1},{1,0},{2,3},{3,2},{4,5},{5,4},{6,7},{7,6},{8,9},{9,8},{10,11... | collective-permute-start | bytes 12296 | tf_op jit(solution)/shard_map/ppermute | solution.py:17
  11.2 3.6 %collective-permute-start.4 = (bf16[4,1,16,128]{3,2,0,1:T(8,128)(2,1)S(1)}, bf16[4,1,16,128]{3,2,0,1:T(8,128)(2,1)S(1)}, u32[]{:S(2)}, u32[]{:S(2)}) collective-permute-start(bf16[4,1,16,128]{3,2,0,1:T(8,128)(2,1)S(1)} %pad_maximum_fusion.4), channel_id=1, source_target_pairs={{0,4},{1,5},{2,6},{3,7},{4,0},{5,1},{6,2},{7,3},{8,12},{9,13},{10,... | collective-permute-start | bytes 49160 | tf_op jit(solution)/shard_map/ppermute | solution.py:17
  16.5 3.2 %collective-permute-start.5 = (bf16[8,1,16,128]{3,2,0,1:T(8,128)(2,1)S(1)}, bf16[8,1,16,128]{3,2,0,1:T(8,128)(2,1)S(1)}, u32[]{:S(2)}, u32[]{:S(2)}) collective-permute-start(bf16[8,1,16,128]{3,2,0,1:T(8,128)(2,1)S(1)} %pad_maximum_fusion.3), channel_id=1, source_target_pairs={{0,8},{1,9},{2,10},{3,11},{4,12},{5,13},{6,14},{7,15},{8,0},{9,1},... | collective-permute-start | bytes 98312 | tf_op jit(solution)/shard_map/ppermute | solution.py:17
  22.8 239.3 %while.28 = (s32[]{:T(128)}, bf16[128,4096]{0,1:T(8,128)(2,1)}, bf16[1,128,4096]{1,2,0:T(8,128)(2,1)}, pred[]{:T(512)}, bf16[1,128,4096]{1,2,0:T(8,128)(2,1)S(1)...) while((s32[]{:T(128)}, bf16[128,4096]{0,1:T(8,128)(2,1)}, ...), condition=%wide.region_5.6_spmd, body=%wide.region_0.5_spmd.sunk | while | flops 82870536 | bytes 83072224 | solution.py:128
  24.0 3.5 %collective-permute-done = bf16[128,4096]{0,1:T(8,128)(2,1)S(1)} collective-permute-done((bf16[128,4096]{0,1:T(8,128)(2,1)}, bf16[128,4096]{0,1:T(8,128)(2,1)S(1)}, u32[]{:S(2)}, u32[]{:S(2)}) %collective-permute-start) | collective-permute-done | bytes 1048608 | tf_op jit(solution)/shard_map/while/body/eval_jaxpr/ppermute | solution.py:31
  27.5 2.7 %fusion.17 = (bf16[128,4096]{0,1:T(8,128)(2,1)S(1)}, bf16[128,4096]{0,1:T(8,128)(2,1)}) fusion(bf16[1,128,4096]{1,2,0:T(8,128)(2,1)} %get-tuple-element.554, bf16[128,4096]{0,1:T(8,128)(2,1)S(1)} %collective-permute-done, bf16[1,128,4096]{1,2,0:T(8,128)(2,1)S(1)} %get-tuple-element.552, pred[]{:T(512)} %get-tuple-element.555), kind=kLoop, calls=%fused_computation.17.clone.1 | loop fusion | flops 2621440 | bytes 5242881 | tf_op jit(solution)/shard_map/while/body/eval_jaxpr/convert_element_type | solution.py:106
  31.5 25.8 %collective-permute-done.1 = bf16[128,4096]{0,1:T(8,128)(2,1)S(1)} collective-permute-done((bf16[128,4096]{0,1:T(8,128)(2,1)S(1)}, bf16[128,4096]{0,1:T(8,128)(2,1)S(1)}, u32[]{:S(2)}, u32[]{:S(2)}) %collective-permute-start.1) | collective-permute-done | bytes 1048608 | tf_op jit(solution)/shard_map/while/body/eval_jaxpr/ppermute | solution.py:31
  57.4 2.7 %fusion.18 = (bf16[1,128,4096]{1,2,0:T(8,128)(2,1)}, bf16[128,4096]{0,1:T(8,128)(2,1)}) fusion(bf16[128,4096]{0,1:T(8,128)(2,1)S(1)} %get-tuple-element.561, bf16[1,128,4096]{1,2,0:T(8,128)(2,1)} %get-tuple-element.537, pred[]{:T(512)S(6)} %and.37, bf16[1,128,4096]{1,2,0:T(8,128)(2,1)S(1)} %get-tuple-element.552, pred[]{:T(512)} %get-tuple-element.551), kind=kLoop, calls=%fused_computation.19.clone.1 | loop fusion | flops 1048576 | bytes 5242882 | tf_op jit(solution)/shard_map/while/body/eval_jaxpr/jit(dynamic_update_index_in_dim)/broadcast_in_dim | solution.py:118
  61.4 84.8 %collective-permute-done = bf16[128,4096]{0,1:T(8,128)(2,1)S(1)} collective-permute-done((bf16[128,4096]{0,1:T(8,128)(2,1)}, bf16[128,4096]{0,1:T(8,128)(2,1)S(1)}, u32[]{:S(2)}, u32[]{:S(2)}) %collective-permute-start) | collective-permute-done | bytes 1048608 | tf_op jit(solution)/shard_map/while/body/eval_jaxpr/ppermute | solution.py:31
  146.2 2.7 %fusion.17 = (bf16[128,4096]{0,1:T(8,128)(2,1)S(1)}, bf16[128,4096]{0,1:T(8,128)(2,1)}) fusion(bf16[1,128,4096]{1,2,0:T(8,128)(2,1)} %get-tuple-element.554, bf16[128,4096]{0,1:T(8,128)(2,1)S(1)} %collective-permute-done, bf16[1,128,4096]{1,2,0:T(8,128)(2,1)S(1)} %get-tuple-element.552, pred[]{:T(512)} %get-tuple-element.555), kind=kLoop, calls=%fused_computation.17.clone.1 | loop fusion | flops 2621440 | bytes 5242881 | tf_op jit(solution)/shard_map/while/body/eval_jaxpr/convert_element_type | solution.py:106
  150.1 25.9 %collective-permute-done.1 = bf16[128,4096]{0,1:T(8,128)(2,1)S(1)} collective-permute-done((bf16[128,4096]{0,1:T(8,128)(2,1)S(1)}, bf16[128,4096]{0,1:T(8,128)(2,1)S(1)}, u32[]{:S(2)}, u32[]{:S(2)}) %collective-permute-start.1) | collective-permute-done | bytes 1048608 | tf_op jit(solution)/shard_map/while/body/eval_jaxpr/ppermute | solution.py:31
  176.1 83.2 %conditional.2 = (bf16[128,4096]{0,1:T(8,128)(2,1)S(1)}) conditional(s32[]{:T(128)} %convert_element_type.55, () %tuple.70, (bf16[128,4096]{0,1:T(8,128)(2,1)}, bf16[16,1,16,128]{3,2,0,1:T(8,128)(2,1)S(1)}, bf16[128,4096]{0,1:T(8,128)(2,1)S(1)}, bf16[128,4096]{0,1:T(8,128)(2,1)S(1)}, s32[1,128]{1,0:T(1,128)S(1)}, /*index=5*/s32[128]{0:T(128)S(1)}) %tuple.71), branch_computations={%region_1.1_spmd, %region_2.4_spmd} | conditional | flops 79200512 | bytes 64197568 | solution.py:116
  177.0 80.3 %while.27 = (s32[]{:T(128)}, f32[4,1,128,64,16]{2,4,3,1,0:T(8,128)}, bf16[4,1,256,64,16]{2,4,3,1,0:T(8,128)(2,1)S(1)}, bf16[4,64,128]{2,1,0:T(8,128)(2,1)S(1)}, ...) while((s32[]{:T(128)}, f32[4,1,128,64,16]{2,4,3,1,0:T(8,128)}, ...), condition=%wide.region_4.3_spmd.clone, body=%wide.region_3.2_spmd.clone.sunk | while | flops 69238784 | bytes 47418224 | solution.py:80
  177.0 3.2 %broadcast_in_dim.57 = bf16[64,128,257]{2,1,0:T(8,128)(2,1)} broadcast(bf16[64,257]{1,0:T(8,128)(2,1)S(1)} %concatenate.30), dimensions={0,2} | broadcast | bytes 4243584 | tf_op jit(solution)/shard_map/while/body/eval_jaxpr/cond/branch_1_fun/while/body/eval_jaxpr/broadcast_in_dim | solution.py:40
  180.2 10.9 %reshape.107 = bf16[64,32896]{1,0:T(8,128)(2,1)} reshape(bf16[64,128,257]{2,1,0:T(8,128)(2,1)} %broadcast_in_dim.57) | data formatting | bytes 8421376 | tf_op jit(solution)/shard_map/while/body/eval_jaxpr/cond/branch_1_fun/while/body/eval_jaxpr/reshape | solution.py:41
  191.1 2.2 slice-done
  197.1 3.2 %broadcast_in_dim.57 = bf16[64,128,257]{2,1,0:T(8,128)(2,1)} broadcast(bf16[64,257]{1,0:T(8,128)(2,1)S(1)} %concatenate.30), dimensions={0,2} | broadcast | bytes 4243584 | tf_op jit(solution)/shard_map/while/body/eval_jaxpr/cond/branch_1_fun/while/body/eval_jaxpr/broadcast_in_dim | solution.py:40
  200.3 10.9 %reshape.107 = bf16[64,32896]{1,0:T(8,128)(2,1)} reshape(bf16[64,128,257]{2,1,0:T(8,128)(2,1)} %broadcast_in_dim.57) | data formatting | bytes 8421376 | tf_op jit(solution)/shard_map/while/body/eval_jaxpr/cond/branch_1_fun/while/body/eval_jaxpr/reshape | solution.py:41
  217.1 3.2 %broadcast_in_dim.57 = bf16[64,128,257]{2,1,0:T(8,128)(2,1)} broadcast(bf16[64,257]{1,0:T(8,128)(2,1)S(1)} %concatenate.30), dimensions={0,2} | broadcast | bytes 4243584 | tf_op jit(solution)/shard_map/while/body/eval_jaxpr/cond/branch_1_fun/while/body/eval_jaxpr/broadcast_in_dim | solution.py:40
  220.3 10.9 %reshape.107 = bf16[64,32896]{1,0:T(8,128)(2,1)} reshape(bf16[64,128,257]{2,1,0:T(8,128)(2,1)} %broadcast_in_dim.57) | data formatting | bytes 8421376 | tf_op jit(solution)/shard_map/while/body/eval_jaxpr/cond/branch_1_fun/while/body/eval_jaxpr/reshape | solution.py:41
  237.2 3.2 %broadcast_in_dim.57 = bf16[64,128,257]{2,1,0:T(8,128)(2,1)} broadcast(bf16[64,257]{1,0:T(8,128)(2,1)S(1)} %concatenate.30), dimensions={0,2} | broadcast | bytes 4243584 | tf_op jit(solution)/shard_map/while/body/eval_jaxpr/cond/branch_1_fun/while/body/eval_jaxpr/broadcast_in_dim | solution.py:40
  240.4 10.9 %reshape.107 = bf16[64,32896]{1,0:T(8,128)(2,1)} reshape(bf16[64,128,257]{2,1,0:T(8,128)(2,1)} %broadcast_in_dim.57) | data formatting | bytes 8421376 | tf_op jit(solution)/shard_map/while/body/eval_jaxpr/cond/branch_1_fun/while/body/eval_jaxpr/reshape | solution.py:41
  259.3 2.7 %fusion.18 = (bf16[1,128,4096]{1,2,0:T(8,128)(2,1)}, bf16[128,4096]{0,1:T(8,128)(2,1)}) fusion(bf16[128,4096]{0,1:T(8,128)(2,1)S(1)} %get-tuple-element.561, bf16[1,128,4096]{1,2,0:T(8,128)(2,1)} %get-tuple-element.537, pred[]{:T(512)S(6)} %and.37, bf16[1,128,4096]{1,2,0:T(8,128)(2,1)S(1)} %get-tuple-element.552, pred[]{:T(512)} %get-tuple-element.551), kind=kLoop, calls=%fused_computation.19.clone.1 | loop fusion | flops 1048576 | bytes 5242882 | tf_op jit(solution)/shard_map/while/body/eval_jaxpr/jit(dynamic_update_index_in_dim)/broadcast_in_dim | solution.py:118
  262.0 2.3 copy.14
  (68 shorter events, 42.9 us)
Async XLA Ops:
  0.0 4.7 %collective-permute-start.2 = (bf16[1,1,16,128]{3,2,0,1:T(8,128)(2,1)}, bf16[1,1,16,128]{3,2,0,1:T(8,128)(2,1)S(1)}, u32[]{:S(2)}, u32[]{:S(2)}) collective-permute-start(bf16[1,1,16,128]{3,2,0,1:T(8,128)(2,1)} %bitcast.86), channel_id=1, source_target_pairs={{0,1},{1,0},{2,3},{3,2},{4,5},{5,4},{6,7},{7,6},{8,9},{9,8},{10,11... | collective-permute-start | bytes 12296 | tf_op jit(solution)/shard_map/ppermute | solution.py:17
  5.4 5.8 %collective-permute-start.3 = (bf16[2,1,16,128]{3,2,0,1:T(8,128)(2,1)S(1)}, bf16[2,1,16,128]{3,2,0,1:T(8,128)(2,1)S(1)}, u32[]{:S(2)}, u32[]{:S(2)}) collective-permute-start(bf16[2,1,16,128]{3,2,0,1:T(8,128)(2,1)S(1)} %pad_maximum_fusion.5), channel_id=1, source_target_pairs={{0,2},{1,3},{2,0},{3,1},{4,6},{5,7},{6,4},{7,5},{8,10},{9,11},{10,... | collective-permute-start | bytes 24584 | tf_op jit(solution)/shard_map/ppermute | solution.py:17
  8.1 13.5 %collective-permute-start.6 = (s32[128]{0:T(128)S(1)}, s32[128]{0:T(128)S(1)}, u32[]{:S(2)}, u32[]{:S(2)}) collective-permute-start(s32[128]{0:T(128)S(1)} %fusion.11), channel_id=1, source_target_pairs={{1,0},{2,1},{3,2},{4,3},{5,4},{6,5},{7,6},{8,7},{9,8},{10,9},{11,1... | collective-permute-start | bytes 1544 | tf_op jit(solution)/shard_map/while/body/eval_jaxpr/ppermute | solution.py:31
  9.4 10.3 %copy-start.1 = (s32[1,128]{1,0:T(1,128)S(1)}, s32[1,128]{1,0:T(1,128)}, u32[]{:S(2)}) copy-start(s32[1,128]{1,0:T(1,128)} %param.12) | copy-start | bytes 1540
  9.5 10.3 %copy-start = (bf16[1,1,128,4096]{3,2,1,0:T(8,128)(2,1)S(1)}, bf16[1,1,128,4096]{3,2,1,0:T(8,128)(2,1)}, u32[]{:S(2)}) copy-start(bf16[1,1,128,4096]{3,2,1,0:T(8,128)(2,1)} %param.10) | copy-start | bytes 3145732
  11.2 5.3 %collective-permute-start.4 = (bf16[4,1,16,128]{3,2,0,1:T(8,128)(2,1)S(1)}, bf16[4,1,16,128]{3,2,0,1:T(8,128)(2,1)S(1)}, u32[]{:S(2)}, u32[]{:S(2)}) collective-permute-start(bf16[4,1,16,128]{3,2,0,1:T(8,128)(2,1)S(1)} %pad_maximum_fusion.4), channel_id=1, source_target_pairs={{0,4},{1,5},{2,6},{3,7},{4,0},{5,1},{6,2},{7,3},{8,12},{9,13},{10,... | collective-permute-start | bytes 49160 | tf_op jit(solution)/shard_map/ppermute | solution.py:17
  16.5 5.1 %collective-permute-start.5 = (bf16[8,1,16,128]{3,2,0,1:T(8,128)(2,1)S(1)}, bf16[8,1,16,128]{3,2,0,1:T(8,128)(2,1)S(1)}, u32[]{:S(2)}, u32[]{:S(2)}) collective-permute-start(bf16[8,1,16,128]{3,2,0,1:T(8,128)(2,1)S(1)} %pad_maximum_fusion.3), channel_id=1, source_target_pairs={{0,8},{1,9},{2,10},{3,11},{4,12},{5,13},{6,14},{7,15},{8,0},{9,1},... | collective-permute-start | bytes 98312 | tf_op jit(solution)/shard_map/ppermute | solution.py:17
  22.8 4.8 %collective-permute-start = (bf16[128,4096]{0,1:T(8,128)(2,1)}, bf16[128,4096]{0,1:T(8,128)(2,1)S(1)}, u32[]{:S(2)}, u32[]{:S(2)}) collective-permute-start(bf16[128,4096]{0,1:T(8,128)(2,1)} %get-tuple-element.536), channel_id=1, source_target_pairs={{16,0},{17,1},{18,2},{19,3},{20,4},{21,5},{22,6},{23,7},{24,8},{25... | collective-permute-start | bytes 3145736 | tf_op jit(solution)/shard_map/while/body/eval_jaxpr/ppermute | solution.py:31
  30.2 27.1 %collective-permute-start.1 = (bf16[128,4096]{0,1:T(8,128)(2,1)S(1)}, bf16[128,4096]{0,1:T(8,128)(2,1)S(1)}, u32[]{:S(2)}, u32[]{:S(2)}) collective-permute-start(bf16[128,4096]{0,1:T(8,128)(2,1)S(1)} %get-tuple-element.489), channel_id=1, source_target_pairs={{1,0},{2,1},{3,2},{4,3},{5,4},{6,5},{7,6},{8,7},{9,8},{10,9},{11,1... | collective-permute-start | bytes 3145736 | tf_op jit(solution)/shard_map/while/body/eval_jaxpr/ppermute | solution.py:31
  60.1 86.0 %collective-permute-start = (bf16[128,4096]{0,1:T(8,128)(2,1)}, bf16[128,4096]{0,1:T(8,128)(2,1)S(1)}, u32[]{:S(2)}, u32[]{:S(2)}) collective-permute-start(bf16[128,4096]{0,1:T(8,128)(2,1)} %get-tuple-element.536), channel_id=1, source_target_pairs={{16,0},{17,1},{18,2},{19,3},{20,4},{21,5},{22,6},{23,7},{24,8},{25... | collective-permute-start | bytes 3145736 | tf_op jit(solution)/shard_map/while/body/eval_jaxpr/ppermute | solution.py:31
  148.8 27.2 %collective-permute-start.1 = (bf16[128,4096]{0,1:T(8,128)(2,1)S(1)}, bf16[128,4096]{0,1:T(8,128)(2,1)S(1)}, u32[]{:S(2)}, u32[]{:S(2)}) collective-permute-start(bf16[128,4096]{0,1:T(8,128)(2,1)S(1)} %get-tuple-element.489), channel_id=1, source_target_pairs={{1,0},{2,1},{3,2},{4,3},{5,4},{6,5},{7,6},{8,7},{9,8},{10,9},{11,1... | collective-permute-start | bytes 3145736 | tf_op jit(solution)/shard_map/while/body/eval_jaxpr/ppermute | solution.py:31
  191.1 2.2 slice-start
  211.2 2.2 slice-start
  231.2 2.2 slice-start
  251.3 2.2 slice-start
